TPU v7x, 32 devices: a whole 2x2x4 slice. The times are simulated.
32 devices in a mesh: shard: 4 (over y, x), replica: 8 (over z, core).
Axes of the slice: x: 2, y: 2, z: 4, core: 2. Of those that a mesh axis runs over, the one named last changes fastest.
Arguments:
- tokens: bfloat16 [2, 8, 1024, 2048], P(None, 'replica', 'shard'), may hold values from -6 to 6
- gain_attn: bfloat16 [2048], P('shard'), may hold values from 0.099609375 to 1.8984375
- w_query: bfloat16 [2048, 2048], P('shard'), may hold values from -0.5 to 0.5
- w_key: bfloat16 [512, 2048], P('shard'), may hold values from -0.5 to 0.5
- w_value: bfloat16 [512, 2048], P('shard'), may hold values from -0.125 to 0.125
- w_out: bfloat16 [2048, 2048], P('shard'), may hold values from -2 to 2
- gain_ff: bfloat16 [2048], P('shard'), may hold values from 0.099609375 to 1.8984375
- w_gate: bfloat16 [8192, 2048], P('shard'), may hold values from -0.125 to 0.125
- w_up: bfloat16 [8192, 2048], P('shard'), may hold values from -0.125 to 0.125
- w_down: bfloat16 [8192, 2048], P('shard'), may hold values from -0.25 to 0.25
- cotangent: bfloat16 [2, 8, 1024, 2048], P(None, 'replica', 'shard'), may hold values from -6 to 6
- segment_ids: int32 [2, 8, 1024], P(None, 'replica', 'shard'), may hold values from 0 to 12, as said below
- parents: int32 [2, 8, 13], P(None, 'replica'), may hold values from 0 to 4, as said below
Outputs:
- output: bfloat16 [2, 8, 1024, 2048], P(None, 'replica', 'shard')
- input_grad: float32 [2, 8, 1024, 2048], P(None, 'replica', 'shard')
- grad_gain_attn: float32 [2048], P('shard')
- grad_query: float32 [2048, 2048], P('shard')
- grad_key: float32 [512, 2048], P('shard')
- grad_value: float32 [512, 2048], P('shard')
- grad_out: float32 [2048, 2048], P('shard')
- grad_gain_ff: float32 [2048], P('shard')
- grad_gate: float32 [8192, 2048], P('shard')
- grad_up: float32 [8192, 2048], P('shard')
- grad_down: float32 [8192, 2048], P('shard')
Inputs may be any that keep to these rules, and one draw needn't show every extreme that they name: `segment_ids`: segment numbers never fall along a tree, begin at 0 (the trunk), and each of the 13 segments holds one token or more. `parents`: segment 0 is its own parent; segments 1 to 4 are children of segment 0; each later segment is a child of one of segments 1 to 4, and every one of those has a child.
All inputs are finite; a program needn't handle non-finite values.
Results may differ from a plain program's by a relative error of at most 0.02.
Values may be sent and summed in bfloat16 or wider, within the bound.
A program may use at most 384 MiB of HBM per device.

v0:
```python
import math
import jax
import jax.numpy as jnp
from jax import lax
from jax.sharding import PartitionSpec as P

HEADS = 32
KV_HEADS = 8
HEAD_DIM = 64
EPSILON = 1e-05
RESIDUAL = 0.22
ATTN_SCALE = 0.015625
ROPE_BASE = 10000000.0
NEGATIVE = -1e30


def tree_layout(segment_row, parent_row):
    seg_numbers = jnp.arange(parent_row.shape[0], dtype=jnp.int32)
    member = (segment_row[:, None] == seg_numbers[None, :]).astype(jnp.int32)
    lengths = jnp.sum(member, axis=0)
    starts = jnp.cumsum(lengths) - lengths
    parent_hit = parent_row[:, None] == seg_numbers[None, :]
    grandparent = jnp.sum(jnp.where(parent_hit, parent_row[None, :], 0), axis=1)
    itself = seg_numbers[:, None] == seg_numbers[None, :]
    related = itself | parent_hit | (grandparent[:, None] == seg_numbers[None, :])
    before = jnp.sum(jnp.where(related & jnp.logical_not(itself), lengths[None, :], 0), axis=1)
    position = jnp.arange(segment_row.shape[0], dtype=jnp.int32) + jnp.dot(member, before - starts)
    return (position, related.astype(jnp.int32), member)


def rotate(values, position, sign):
    half = values.shape[-1] // 2
    fraction = jnp.arange(half, dtype=jnp.float32) * (2.0 / values.shape[-1])
    freq = jnp.exp(-math.log(ROPE_BASE) * fraction)
    angle = position.astype(jnp.float32)[:, None] * freq[None, :]
    cosine = jnp.concatenate([jnp.cos(angle), jnp.cos(angle)], axis=-1)[:, None, :]
    sine = jnp.concatenate([jnp.sin(angle), jnp.sin(angle)], axis=-1)[:, None, :]
    turned = jnp.concatenate([-values[..., half:], values[..., :half]], axis=-1)
    return values * cosine + sign * turned * sine


def contract_last(left, right):
    return lax.dot_general(
        left, right, (((1,), (1,)), ((), ())), preferred_element_type=jnp.float32
    )


def contract_first(left, right):
    return lax.dot_general(
        left, right, (((0,), (0,)), ((), ())), preferred_element_type=jnp.float32
    )


def norm_back(values, scale, gain, grad_in):
    scaled = values * scale
    weighted = grad_in * gain
    back = scale * (weighted - scaled * jnp.mean(weighted * scaled, axis=-1, keepdims=True))
    return (back, jnp.sum(grad_in * scaled, axis=0))


def block_mask(member, related, begin, block_rows):
    member_block = lax.slice_in_dim(member, begin, begin + block_rows, axis=0)
    link = jnp.dot(jnp.dot(member_block, related), member.T)
    query_index = begin + jnp.arange(block_rows, dtype=jnp.int32)
    key_index = jnp.arange(member.shape[0], dtype=jnp.int32)
    return ((link > 0) & (key_index[None, :] <= query_index[:, None]))[None, None]


def body(
    tokens,
    gain_attn,
    w_query,
    w_key,
    w_value,
    w_out,
    gain_ff,
    w_gate,
    w_up,
    w_down,
    cotangent,
    segment_ids,
    parents,
):
    width = tokens.shape[3]
    group = HEADS // KV_HEADS
    all_segments = lax.all_gather(segment_ids, "shard", axis=2, tiled=True)
    tree_rows = all_segments.shape[2]
    block_rows = min(512, tree_rows)
    sums = [
        jnp.zeros(w.shape, jnp.float32)
        for w in (gain_attn, w_query, w_key, w_value, w_out, gain_ff, w_gate, w_up, w_down)
    ]
    gains = (
        lax.all_gather(gain_attn, "shard", axis=0, tiled=True),
        lax.all_gather(gain_ff, "shard", axis=0, tiled=True),
    )
    gain_first = gains[0].astype(jnp.float32)
    gain_second = gains[1].astype(jnp.float32)
    gain_attn_acc = jnp.zeros((width,), jnp.float32)
    gain_ff_acc = jnp.zeros((width,), jnp.float32)
    results = []
    input_grads = []
    for batch_index in range(tokens.shape[0]):
        inputs = tokens[batch_index, 0].astype(jnp.float32)
        position_all, related, member = tree_layout(
            all_segments[batch_index, 0], parents[batch_index, 0]
        )
        scale_first = lax.rsqrt(jnp.mean(inputs * inputs, axis=-1, keepdims=True) + EPSILON)
        normed = (inputs * scale_first * gain_first).astype(jnp.bfloat16)
        normed_all = lax.all_gather(normed, "shard", axis=0, tiled=True)
        own_heads = w_key.shape[0] // HEAD_DIM
        query_h = rotate(
            contract_last(normed_all, w_query).reshape(tree_rows, own_heads * group, HEAD_DIM),
            position_all,
            1.0,
        )
        query_h = query_h.astype(jnp.bfloat16).reshape(tree_rows, own_heads, group, HEAD_DIM)
        key_h = rotate(
            contract_last(normed_all, w_key).reshape(tree_rows, own_heads, HEAD_DIM),
            position_all,
            1.0,
        ).astype(jnp.bfloat16)
        value_h = (
            contract_last(normed_all, w_value)
            .astype(jnp.bfloat16)
            .reshape(tree_rows, own_heads, HEAD_DIM)
        )
        masks = []
        log_totals = []
        pieces = []
        for begin in range(0, tree_rows, block_rows):
            allowed_blk = block_mask(member, related, begin, block_rows)
            query_blk = query_h[begin : begin + block_rows]
            scores = (
                jnp.einsum("qhgd,khd->hgqk", query_blk, key_h, preferred_element_type=jnp.float32)
                * ATTN_SCALE
            )
            masked = jnp.where(allowed_blk, scores, NEGATIVE)
            top = jnp.max(masked, axis=-1, keepdims=True)
            expo = jnp.exp(masked - top)
            total = jnp.sum(expo, axis=-1, keepdims=True)
            masks.append(allowed_blk)
            log_totals.append(top + jnp.log(total))
            probs_low = (expo / total).astype(jnp.bfloat16)
            mixed = jnp.einsum(
                "hgqk,khd->qhgd", probs_low, value_h, preferred_element_type=jnp.float32
            )
            pieces.append(mixed.reshape(block_rows, own_heads * group * HEAD_DIM))
        attended_h = jnp.concatenate(pieces, axis=0).astype(jnp.bfloat16)
        attn_branch = lax.psum_scatter(
            jnp.dot(attended_h, w_out, preferred_element_type=jnp.float32),
            "shard",
            scatter_dimension=0,
            tiled=True,
        )
        middle = inputs + RESIDUAL * attn_branch
        scale_second = lax.rsqrt(jnp.mean(middle * middle, axis=-1, keepdims=True) + EPSILON)
        normed_ff = (middle * scale_second * gain_second).astype(jnp.bfloat16)
        rows_all = lax.all_gather(normed_ff, "shard", axis=0, tiled=True)
        gate = contract_last(rows_all, w_gate)
        upper = contract_last(rows_all, w_up)
        hidden = (gate * jax.nn.sigmoid(gate) * upper).astype(jnp.bfloat16)
        down_branch = lax.psum_scatter(
            jnp.dot(hidden, w_down, preferred_element_type=jnp.float32).astype(jnp.bfloat16),
            "shard",
            scatter_dimension=0,
            tiled=True,
        ).astype(jnp.float32)
        results.append((middle + RESIDUAL * down_branch).astype(jnp.bfloat16))
        cot = cotangent[batch_index, 0].astype(jnp.float32)
        down_grad = (RESIDUAL * cot).astype(jnp.bfloat16)
        cot_all = lax.all_gather(down_grad, "shard", axis=0, tiled=True)
        gate = contract_last(rows_all, w_gate)
        upper = contract_last(rows_all, w_up)
        sigma = jax.nn.sigmoid(gate)
        hidden = (gate * sigma * upper).astype(jnp.bfloat16)
        hidden_grad = contract_last(cot_all, w_down)
        gate_grad = (hidden_grad * upper * sigma * (1.0 + gate * (1.0 - sigma))).astype(
            jnp.bfloat16
        )
        up_grad = (hidden_grad * gate * sigma).astype(jnp.bfloat16)
        sums[6] = sums[6] + contract_first(gate_grad, rows_all)
        sums[7] = sums[7] + contract_first(up_grad, rows_all)
        sums[8] = sums[8] + contract_first(hidden, cot_all)
        ff_normed_grad = lax.psum_scatter(
            jnp.dot(gate_grad, w_gate, preferred_element_type=jnp.float32)
            + jnp.dot(up_grad, w_up, preferred_element_type=jnp.float32),
            "shard",
            scatter_dimension=0,
            tiled=True,
        )
        middle_back, gain_ff_term = norm_back(middle, scale_second, gain_second, ff_normed_grad)
        middle_grad = cot + middle_back
        out_grad = (RESIDUAL * middle_grad).astype(jnp.bfloat16)
        out_all = lax.all_gather(out_grad, "shard", axis=0, tiled=True)
        sums[4] = sums[4] + contract_first(attended_h, out_all)
        attended_grad = (
            contract_last(out_all, w_out)
            .astype(jnp.bfloat16)
            .reshape(tree_rows, own_heads, group, HEAD_DIM)
        )
        value_term = jnp.zeros((tree_rows, own_heads, HEAD_DIM), jnp.float32)
        key_term = jnp.zeros((tree_rows, own_heads, HEAD_DIM), jnp.float32)
        query_parts = []
        for block_index, begin in enumerate(range(0, tree_rows, block_rows)):
            query_blk = query_h[begin : begin + block_rows]
            grad_blk = attended_grad[begin : begin + block_rows]
            scores = (
                jnp.einsum("qhgd,khd->hgqk", query_blk, key_h, preferred_element_type=jnp.float32)
                * ATTN_SCALE
            )
            probs = jnp.exp(
                jnp.where(masks[block_index], scores, NEGATIVE) - log_totals[block_index]
            )
            probs_low = probs.astype(jnp.bfloat16)
            probs_grad = jnp.einsum(
                "qhgd,khd->hgqk", grad_blk, value_h, preferred_element_type=jnp.float32
            )
            value_term = value_term + jnp.einsum(
                "hgqk,qhgd->khd", probs_low, grad_blk, preferred_element_type=jnp.float32
            )
            score_grad = (
                probs * (probs_grad - jnp.sum(probs_grad * probs, axis=-1, keepdims=True))
            ).astype(jnp.bfloat16)
            query_parts.append(
                jnp.einsum("hgqk,khd->qhgd", score_grad, key_h, preferred_element_type=jnp.float32)
                * ATTN_SCALE
            )
            key_term = (
                key_term
                + jnp.einsum(
                    "hgqk,qhgd->khd", score_grad, query_blk, preferred_element_type=jnp.float32
                )
                * ATTN_SCALE
            )
        query_grad = jnp.concatenate(query_parts, axis=0)
        query_raw = rotate(
            query_grad.reshape(tree_rows, own_heads * group, HEAD_DIM), position_all, -1.0
        )
        query_raw = query_raw.reshape(tree_rows, own_heads * group * HEAD_DIM).astype(jnp.bfloat16)
        key_raw = (
            rotate(key_term, position_all, -1.0)
            .reshape(tree_rows, own_heads * HEAD_DIM)
            .astype(jnp.bfloat16)
        )
        value_raw = value_term.reshape(tree_rows, own_heads * HEAD_DIM).astype(jnp.bfloat16)
        sums[1] = sums[1] + contract_first(query_raw, normed_all)
        sums[2] = sums[2] + contract_first(key_raw, normed_all)
        sums[3] = sums[3] + contract_first(value_raw, normed_all)
        normed_grad = lax.psum_scatter(
            (
                jnp.dot(query_raw, w_query, preferred_element_type=jnp.float32)
                + jnp.dot(key_raw, w_key, preferred_element_type=jnp.float32)
                + jnp.dot(value_raw, w_value, preferred_element_type=jnp.float32)
            ).astype(jnp.bfloat16),
            "shard",
            scatter_dimension=0,
            tiled=True,
        ).astype(jnp.float32)
        input_back, gain_attn_term = norm_back(inputs, scale_first, gain_first, normed_grad)
        input_grads.append(middle_grad + input_back)
        gain_attn_acc = gain_attn_acc + gain_attn_term
        gain_ff_acc = gain_ff_acc + gain_ff_term
    owned_gains = (
        lax.psum_scatter(gain_attn_acc, "shard", scatter_dimension=0, tiled=True),
        lax.psum_scatter(gain_ff_acc, "shard", scatter_dimension=0, tiled=True),
    )
    sums[0] = owned_gains[0]
    sums[5] = owned_gains[1]
    totals = (
        lax.psum(sums[0].astype(jnp.bfloat16), "replica").astype(jnp.float32),
        lax.psum(sums[1].astype(jnp.bfloat16), "replica").astype(jnp.float32),
        lax.psum(sums[2].astype(jnp.bfloat16), "replica").astype(jnp.float32),
        lax.psum(sums[3].astype(jnp.bfloat16), "replica").astype(jnp.float32),
        lax.psum(sums[4].astype(jnp.bfloat16), "replica").astype(jnp.float32),
        lax.psum(sums[5].astype(jnp.bfloat16), "replica").astype(jnp.float32),
        lax.psum(sums[6].astype(jnp.bfloat16), "replica").astype(jnp.float32),
        lax.psum(sums[7].astype(jnp.bfloat16), "replica").astype(jnp.float32),
        lax.psum(sums[8].astype(jnp.bfloat16), "replica").astype(jnp.float32),
    )
    output = jnp.stack(results)[:, None]
    input_grad = jnp.stack(input_grads)[:, None]
    return (
        output,
        input_grad,
        totals[0],
        totals[1],
        totals[2],
        totals[3],
        totals[4],
        totals[5],
        totals[6],
        totals[7],
        totals[8],
    )


def solution(mesh):
    in_specs = (
        P(None, "replica", "shard", None),
        P("shard"),
        P("shard", None),
        P("shard", None),
        P("shard", None),
        P("shard", None),
        P("shard"),
        P("shard", None),
        P("shard", None),
        P("shard", None),
        P(None, "replica", "shard", None),
        P(None, "replica", "shard"),
        P(None, "replica", None),
    )
    out_specs = (
        P(None, "replica", "shard", None),
        P(None, "replica", "shard", None),
        P("shard"),
        P("shard", None),
        P("shard", None),
        P("shard", None),
        P("shard", None),
        P("shard"),
        P("shard", None),
        P("shard", None),
        P("shard", None),
    )
    return jax.shard_map(body, mesh=mesh, in_specs=in_specs, out_specs=out_specs, check_vma=False)
```

profile of v0, /device:TPU:0, one launch (start us, length us, event | category | flops | bytes accessed | tf_op | source)
XLA Modules:
  0.0 1901.9 jit_solution(17890299135495085045)
XLA Ops:
  44.1 32.7 %all-gather.15.cloned.1.call-done = bf16[1024,2048]{1,0:T(8,128)(2,1)} async-done(((bf16[256,2048]{1,0:T(8,128)(2,1)}), bf16[1024,2048]{1,0:T(8,128)(2,1)}) %all-gather.15.cloned.1.call-update) | async-done | bytes 4194320 | tf_op jit(solution)/shard_map/all_gather | solution.py:110
  229.1 89.6 %reduce-scatter.9.cloned.1.call-done = f32[256,2048]{1,0:T(8,128)} async-done(((f32[1024,2048]{1,0:T(8,128)}), f32[256,2048]{1,0:T(8,128)}) %reduce-scatter.9.cloned.1.call-update) | async-done | bytes 2097168 | tf_op jit(solution)/shard_map/reduce_scatter | solution.py:150
  329.8 49.3 %all-gather.13.cloned.1.call-done = bf16[1024,2048]{1,0:T(8,128)(2,1)} async-done(((bf16[256,2048]{1,0:T(8,128)(2,1)}), bf16[1024,2048]{1,0:T(8,128)(2,1)}) %all-gather.13.cloned.1.call-update) | async-done | bytes 4194320 | tf_op jit(solution)/shard_map/all_gather | solution.py:159
  379.1 15.9 fusion.186
  408.2 25.9 %all-gather.19.cloned.1.call-done = bf16[1024,2048]{1,0:T(8,128)(2,1)} async-done(((bf16[256,2048]{1,0:T(8,128)(2,1)}), bf16[1024,2048]{1,0:T(8,128)(2,1)}) %all-gather.19.cloned.1.call-update) | async-done | bytes 4194320 | tf_op jit(solution)/shard_map/all_gather | solution.py:172
  434.1 22.0 %multiply_convert_fusion.2 = (bf16[1024,2048]{1,0:T(8,128)(2,1)}, bf16[1024,2048]{1,0:T(8,128)(2,1)}, bf16[1024,2048]{1,0:T(8,128)(2,1)}) fusion(f32[1024,2048]{1,0:T(8,128)} %fusion.185, f32[1024,2048]{1,0:T(8,128)} %fusion.186, bf16[1024,2048]{1,0:T(8,128)(2,1)} %all-gather.19.cloned.1.call-done, bf16[2048,2048]{1,0:T(8,128)(2,1)} %param.22), kind=kOutput, calls=%fused_computation.59 | convolution fusion | flops 8623489024 | bytes 41943040 | tf_op jit(solution)/shard_map/dot_general | solution.py:43
  482.2 86.3 %reduce-scatter.17.cloned.1.call-done = f32[256,2048]{1,0:T(8,128)} async-done(((f32[1024,2048]{1,0:T(8,128)}), f32[256,2048]{1,0:T(8,128)}) %reduce-scatter.17.cloned.1.call-update) | async-done | bytes 2097168 | tf_op jit(solution)/shard_map/reduce_scatter | solution.py:185
  574.4 52.1 %all-gather.17.cloned.1.call-done = bf16[1024,2048]{1,0:T(8,128)(2,1)} async-done(((bf16[256,2048]{1,0:T(8,128)(2,1)}), bf16[1024,2048]{1,0:T(8,128)(2,1)}) %all-gather.17.cloned.1.call-update) | async-done | bytes 4194320 | tf_op jit(solution)/shard_map/all_gather | solution.py:159
  626.4 15.5 fusion.190
  655.1 26.0 %all-gather.23.cloned.1.call-done = bf16[1024,2048]{1,0:T(8,128)(2,1)} async-done(((bf16[256,2048]{1,0:T(8,128)(2,1)}), bf16[1024,2048]{1,0:T(8,128)(2,1)}) %all-gather.23.cloned.1.call-update) | async-done | bytes 4194320 | tf_op jit(solution)/shard_map/all_gather | solution.py:172
  681.2 22.3 %multiply_convert_fusion = (bf16[1024,2048]{1,0:T(8,128)(2,1)}, bf16[1024,2048]{1,0:T(8,128)(2,1)}, bf16[1024,2048]{1,0:T(8,128)(2,1)}) fusion(f32[1024,2048]{1,0:T(8,128)} %fusion.189, f32[1024,2048]{1,0:T(8,128)} %fusion.190, bf16[1024,2048]{1,0:T(8,128)(2,1)} %all-gather.23.cloned.1.call-done, bf16[2048,2048]{1,0:T(8,128)(2,1)} %param.22), kind=kOutput, calls=%fused_computation.54 | convolution fusion | flops 8623489024 | bytes 41943040 | tf_op jit(solution)/shard_map/dot_general | solution.py:43
  729.4 14.0 convolution_convert_fusion
  743.5 72.4 %reduce-scatter.21.cloned.1.call-done = f32[256,2048]{1,0:T(8,128)} async-done(((f32[1024,2048]{1,0:T(8,128)}), f32[256,2048]{1,0:T(8,128)}) %reduce-scatter.21.cloned.1.call-update) | async-done | bytes 2097168 | tf_op jit(solution)/shard_map/reduce_scatter | solution.py:185
  819.4 52.2 %reduce-scatter.15.cloned.1.call-done = bf16[256,2048]{1,0:T(8,128)(2,1)} async-done(((bf16[1024,2048]{1,0:T(8,128)(2,1)}), bf16[256,2048]{1,0:T(8,128)(2,1)}) %reduce-scatter.15.cloned.1.call-update) | async-done | bytes 1048592 | tf_op jit(solution)/shard_map/reduce_scatter | solution.py:163
  878.8 52.0 %all-gather.21.cloned.1.call-done = bf16[1024,2048]{1,0:T(8,128)(2,1)} async-done(((bf16[256,2048]{1,0:T(8,128)(2,1)}), bf16[1024,2048]{1,0:T(8,128)(2,1)}) %all-gather.21.cloned.1.call-update) | async-done | bytes 4194320 | tf_op jit(solution)/shard_map/all_gather | solution.py:195
  1030.9 15.0 fusion
  1135.3 14.2 convolution_convert_fusion.1
  1149.6 15.8 fusion.202
  1188.9 16.2 add_convert_fusion
  1205.1 16.1 add_convert_fusion.1
  1221.2 16.3 add_convert_fusion.2
  1261.2 15.1 all-reduce.2
  1276.4 14.6 all-reduce.3
  1302.7 547.4 %all-reduce.7.cloned.1.call-done = (bf16[512,2048]{1,0:T(8,128)(2,1)}, bf16[128,2048]{1,0:T(8,128)(2,1)}, bf16[128,2048]{1,0:T(8,128)(2,1)}, bf16[512,2048]{1,0:...) async-done(((bf16[512,2048]{1,0:T(8,128)(2,1)}, bf16[128,2048]{1,0:T(8,128)(2,1)}, bf16[128,2048]{1,0:T(8,128)(2,1)}, ...) | async-done | bytes 30408720 | tf_op jit(solution)/shard_map/psum | solution.py:272
  (520 shorter events, 586.0 us)
Async XLA Ops:
  7.2 129.6 %copy-start = (bf16[512,2048]{1,0:T(8,128)(2,1)S(1)}, bf16[512,2048]{1,0:T(8,128)(2,1)}, u32[]{:S(2)}) copy-start(bf16[512,2048]{1,0:T(8,128)(2,1)} %param.18) | copy-start | bytes 6291460
  7.2 69.6 %all-gather.15.cloned.1.call-start = ((), (), s32[]{:S(2)}) async-start(), calls=%async_computation.12 | async-start | bytes 5242880 | tf_op jit(solution)/shard_map/all_gather | solution.py:110
  23.7 131.5 %all-gather.11.cloned.1.call-start = ((), (), s32[]{:S(2)}) async-start(), calls=%async_computation.8 | async-start | bytes 5242880 | tf_op jit(solution)/shard_map/all_gather | solution.py:110
  24.4 204.7 %reduce-scatter.13.cloned.1.call-start = ((), (), s32[]{:S(2)}) async-start(), calls=%async_computation.13 | async-start | bytes 10485760 | tf_op jit(solution)/shard_map/reduce_scatter | solution.py:150
  142.5 176.3 %reduce-scatter.9.cloned.1.call-start = ((), (), s32[]{:S(2)}) async-start(), calls=%async_computation.9 | async-start | bytes 10485760 | tf_op jit(solution)/shard_map/reduce_scatter | solution.py:150
  217.2 161.8 %all-gather.13.cloned.1.call-start = ((), (), s32[]{:S(2)}) async-start(), calls=%async_computation.10 | async-start | bytes 5242880 | tf_op jit(solution)/shard_map/all_gather | solution.py:159
  225.9 645.8 %copy-start.68 = (f32[4,1,512]{2,1,0:T(1,128)}, f32[4,1,512]{2,1,0:T(1,128)S(1)}, u32[]{:S(2)}) copy-start(f32[4,1,512]{2,1,0:T(1,128)S(1)} %convert_element_type.369) | copy-start | bytes 24580
  323.7 548.0 %copy-start.91 = (f32[256]{0:T(256)}, f32[256]{0:T(256)S(1)}, u32[]{:S(2)}) copy-start(f32[256]{0:T(256)S(1)} %add_rsqrt_fusion.2) | copy-start | bytes 3076
  326.2 107.8 %all-gather.19.cloned.1.call-start = ((), (), s32[]{:S(2)}) async-start(), calls=%async_computation.16 | async-start | bytes 5242880 | tf_op jit(solution)/shard_map/all_gather | solution.py:172
  329.7 238.8 %reduce-scatter.17.cloned.1.call-start = ((), (), s32[]{:S(2)}) async-start(), calls=%async_computation.17 | async-start | bytes 10485760 | tf_op jit(solution)/shard_map/reduce_scatter | solution.py:185
  481.9 144.6 %all-gather.17.cloned.1.call-start = ((), (), s32[]{:S(2)}) async-start(), calls=%async_computation.14 | async-start | bytes 5242880 | tf_op jit(solution)/shard_map/all_gather | solution.py:159
  482.2 389.5 %copy-start.89 = (f32[256]{0:T(256)}, f32[256]{0:T(256)S(1)}, u32[]{:S(2)}) copy-start(f32[256]{0:T(256)S(1)} %add_rsqrt_fusion) | copy-start | bytes 3076
  573.6 107.6 %all-gather.23.cloned.1.call-start = ((), (), s32[]{:S(2)}) async-start(), calls=%async_computation.20 | async-start | bytes 5242880 | tf_op jit(solution)/shard_map/all_gather | solution.py:172
  574.3 241.6 %reduce-scatter.21.cloned.1.call-start = ((), (), s32[]{:S(2)}) async-start(), calls=%async_computation.21 | async-start | bytes 10485760 | tf_op jit(solution)/shard_map/reduce_scatter | solution.py:185
  729.4 142.2 %reduce-scatter.15.cloned.1.call-start = ((), (), s32[]{:S(2)}) async-start(), calls=%async_computation.15 | async-start | bytes 5242880 | tf_op jit(solution)/shard_map/reduce_scatter | solution.py:163
  743.5 187.4 %all-gather.21.cloned.1.call-start = ((), (), s32[]{:S(2)}) async-start(), calls=%async_computation.18 | async-start | bytes 5242880 | tf_op jit(solution)/shard_map/all_gather | solution.py:195
  743.5 134.4 %copy-start.99 = (f32[256]{0:T(256)}, f32[256]{0:T(256)S(1)}, u32[]{:S(2)}) copy-start(f32[256]{0:T(256)S(1)} %broadcast_multiply_fusion.9) | copy-start | bytes 3076
  819.4 58.7 %copy-start.79 = (f32[2,4,512]{2,1,0:T(4,128)S(1)}, f32[2,4,512]{2,1,0:T(4,128)}, u32[]{:S(2)}) copy-start(f32[2,4,512]{2,1,0:T(4,128)} %copy-done.78) | copy-start | bytes 49156
  819.4 58.7 %copy-start.84 = (f32[2,4,512]{2,1,0:T(4,128)S(1)}, f32[2,4,512]{2,1,0:T(4,128)}, u32[]{:S(2)}) copy-start(f32[2,4,512]{2,1,0:T(4,128)} %copy-done.83) | copy-start | bytes 49156
  878.0 108.2 %all-gather.25.cloned.1.call-start = ((), (), s32[]{:S(2)}) async-start(), calls=%async_computation.22 | async-start | bytes 5242880 | tf_op jit(solution)/shard_map/all_gather | solution.py:195
  878.7 379.5 %reduce-scatter.19.cloned.1.call-start = ((), (), s32[]{:S(2)}) async-start(), calls=%async_computation.19 | async-start | bytes 5242880 | tf_op jit(solution)/shard_map/reduce_scatter | solution.py:250
  1029.9 228.3 %reduce-scatter.23.cloned.1.call-start = ((), (), s32[]{:S(2)}) async-start(), calls=%async_computation.23 | async-start | bytes 5242880 | tf_op jit(solution)/shard_map/reduce_scatter | solution.py:250
  1135.2 156.9 %reduce-scatter.11.cloned.1.call-start = ((), (), s32[]{:S(2)}) async-start(), calls=%async_computation.11 | async-start | bytes 5242880 | tf_op jit(solution)/shard_map/reduce_scatter | solution.py:163
  1149.5 700.6 %all-reduce.7.cloned.1.call-start = ((), (), s32[]{:S(2)}) async-start(), calls=%async_computation.24 | async-start | bytes 60817408 | tf_op jit(solution)/shard_map/psum | solution.py:272
  (149 other events, 1669.5 us)
Sparse Core Ops, SparseCore 0:
  23.8 52.9 all-gather.14
  79.2 52.6 all-gather.10
  142.6 86.4 reduce-scatter.12
  232.4 86.3 reduce-scatter.8
  326.3 52.6 all-gather.12
  381.3 52.6 all-gather.18
  482.0 86.4 reduce-scatter.16
  573.7 52.6 all-gather.16
  628.4 52.6 all-gather.22
  729.5 86.4 reduce-scatter.20
  818.9 52.6 reduce-scatter.14
  878.1 52.6 all-gather.20
  933.4 52.6 all-gather.24
  1030.1 52.6 reduce-scatter.18
  1135.4 52.6 reduce-scatter.22
  1191.2 52.6 reduce-scatter.10
  1256.5 593.6 all-reduce.6
where the time goes:
time: 1910 us; the launch traced here: 1900 us
  waiting for transfers between devices  1100 us (58%)
  matrix products  510 us (27%)
  other arithmetic  179 us (9%)
  blocking collectives  55.1 us (3%)
  local copies, waits for them, and re-layouts  39.5 us (2%)
    psum x1, waiting for transfers between devices, body(): lax.psum(sums[1].astype(jnp.bfloat16), 'replica').astype(jnp.float32)  547 us
    reduce_scatter x2, waiting for transfers between devices, body(): lax.psum_scatter(jnp.dot(gate_grad, w_gate, preferred_element_type=jnp.fl...  159 us
    dot_general x14, matrix products, contract_last(): lax.dot_general(left, right, (((1,), (1,)), ((), ())), preferred_element_...  129 us
    dot_general x14, matrix products, contract_first(): lax.dot_general(left, right, (((0,), (0,)), ((), ())), preferred_element_...  104 us
    all_gather x2, waiting for transfers between devices, body(): rows_all = lax.all_gather(normed_ff, 'shard', axis=0, tiled=True)  101 us
    reduce_scatter x2, waiting for transfers between devices, body(): lax.psum_scatter(jnp.dot(attended_h, w_out, preferred_element_type=jnp.fl...  92.9 us
    all_gather x2, waiting for transfers between devices, body(): out_all = lax.all_gather(out_grad, 'shard', axis=0, tiled=True)  61 us
    reduce_scatter x2, waiting for transfers between devices, body(): lax.psum_scatter(jnp.dot(hidden, w_down, preferred_element_type=jnp.float...  52.2 us
  transfers between devices with their start and end apart: 17, of which 13 were waited for; matrix products, arithmetic and copies ran while one was open for 26% of the time, Pallas kernels for 0%

commit v1 on v0

--- a/solution.py
+++ b/solution.py
@@ -81,6 +81,11 @@
     segment_ids,
     parents,
 ):
+
+    def targets_set(buf):
+        all_rows = jax.lax.all_gather(buf, axis_name="replica")
+        return jnp.sum(all_rows, 0)
+
     width = tokens.shape[3]
     group = HEADS // KV_HEADS
     all_segments = lax.all_gather(segment_ids, "shard", axis=2, tiled=True)
@@ -269,7 +274,7 @@
     sums[5] = owned_gains[1]
     totals = (
         lax.psum(sums[0].astype(jnp.bfloat16), "replica").astype(jnp.float32),
-        lax.psum(sums[1].astype(jnp.bfloat16), "replica").astype(jnp.float32),
+        targets_set(sums[1].astype(jnp.bfloat16)).astype(jnp.float32),
         lax.psum(sums[2].astype(jnp.bfloat16), "replica").astype(jnp.float32),
         lax.psum(sums[3].astype(jnp.bfloat16), "replica").astype(jnp.float32),
         lax.psum(sums[4].astype(jnp.bfloat16), "replica").astype(jnp.float32),

time: 1910 us -> 1980 us (1.037)
  waiting for transfers between devices: 1100 us -> 1160 us
    all_gather x0 -> x1, waiting for transfers between devices: none -> 110 us  [targets_set(): all_rows = jax.lax.all_gather(buf, axis_name='replica')]
    psum x1, waiting for transfers between devices: 547 us -> 498 us  [body(): lax.psum(sums[2].astype(jnp.bfloat16), 'replica').astype(jnp.float32)]
  transfers between devices with their start and end apart: 17 -> 18, of which waited for: 13 -> 14; matrix products, arithmetic and copies ran while one was open for 26% -> 27% of each run, Pallas kernels for 0% -> 0%
where the time goes in v1:
time: 1980 us
  waiting for transfers between devices  1160 us (59%)
  matrix products  512 us (26%)
  other arithmetic  192 us (10%)
  blocking collectives  55.3 us (3%)
  local copies, waits for them, and re-layouts  40 us (2%)
    psum x1, waiting for transfers between devices, body(): lax.psum(sums[2].astype(jnp.bfloat16), 'replica').astype(jnp.float32)  498 us
    reduce_scatter x2, waiting for transfers between devices, body(): lax.psum_scatter(jnp.dot(gate_grad, w_gate, preferred_element_type=jnp.fl...  159 us
    dot_general x14, matrix products, contract_last(): lax.dot_general(left, right, (((1,), (1,)), ((), ())), preferred_element_...  129 us
    all_gather x1, waiting for transfers between devices, targets_set(): all_rows = jax.lax.all_gather(buf, axis_name='replica')  110 us
    dot_general x14, matrix products, contract_first(): lax.dot_general(left, right, (((0,), (0,)), ((), ())), preferred_element_...  107 us
    all_gather x2, waiting for transfers between devices, body(): rows_all = lax.all_gather(normed_ff, 'shard', axis=0, tiled=True)  101 us
    reduce_scatter x2, waiting for transfers between devices, body(): lax.psum_scatter(jnp.dot(attended_h, w_out, preferred_element_type=jnp.fl...  92.9 us
    all_gather x2, waiting for transfers between devices, body(): out_all = lax.all_gather(out_grad, 'shard', axis=0, tiled=True)  61.3 us
  transfers between devices with their start and end apart: 18, of which 14 were waited for; matrix products, arithmetic and copies ran while one was open for 27% of the time, Pallas kernels for 0%

profile of v1, /device:TPU:0, one launch (start us, length us, event | category | flops | bytes accessed | tf_op | source)
XLA Modules:
  0.0 1979.4 jit_solution(11353267896459230729)
XLA Ops:
  44.1 32.7 %all-gather.17.cloned.1.call-done = bf16[1024,2048]{1,0:T(8,128)(2,1)} async-done(((bf16[256,2048]{1,0:T(8,128)(2,1)}), bf16[1024,2048]{1,0:T(8,128)(2,1)}) %all-gather.17.cloned.1.call-update) | async-done | bytes 4194320 | tf_op jit(solution)/shard_map/all_gather | solution.py:115
  229.0 89.6 %reduce-scatter.9.cloned.1.call-done = f32[256,2048]{1,0:T(8,128)} async-done(((f32[1024,2048]{1,0:T(8,128)}), f32[256,2048]{1,0:T(8,128)}) %reduce-scatter.9.cloned.1.call-update) | async-done | bytes 2097168 | tf_op jit(solution)/shard_map/reduce_scatter | solution.py:155
  329.6 49.3 %all-gather.15.cloned.1.call-done = bf16[1024,2048]{1,0:T(8,128)(2,1)} async-done(((bf16[256,2048]{1,0:T(8,128)(2,1)}), bf16[1024,2048]{1,0:T(8,128)(2,1)}) %all-gather.15.cloned.1.call-update) | async-done | bytes 4194320 | tf_op jit(solution)/shard_map/all_gather | solution.py:164
  378.9 15.7 fusion.186
  407.9 26.1 %all-gather.21.cloned.1.call-done = bf16[1024,2048]{1,0:T(8,128)(2,1)} async-done(((bf16[256,2048]{1,0:T(8,128)(2,1)}), bf16[1024,2048]{1,0:T(8,128)(2,1)}) %all-gather.21.cloned.1.call-update) | async-done | bytes 4194320 | tf_op jit(solution)/shard_map/all_gather | solution.py:177
  433.9 22.3 %multiply_convert_fusion.2 = (bf16[1024,2048]{1,0:T(8,128)(2,1)}, bf16[1024,2048]{1,0:T(8,128)(2,1)}, bf16[1024,2048]{1,0:T(8,128)(2,1)}) fusion(f32[1024,2048]{1,0:T(8,128)} %fusion.185, f32[1024,2048]{1,0:T(8,128)} %fusion.186, bf16[1024,2048]{1,0:T(8,128)(2,1)} %all-gather.21.cloned.1.call-done, bf16[2048,2048]{1,0:T(8,128)(2,1)} %param.22), kind=kOutput, calls=%fused_computation.59 | convolution fusion | flops 8623489024 | bytes 41943040 | tf_op jit(solution)/shard_map/dot_general | solution.py:43
  482.2 86.3 %reduce-scatter.17.cloned.1.call-done = f32[256,2048]{1,0:T(8,128)} async-done(((f32[1024,2048]{1,0:T(8,128)}), f32[256,2048]{1,0:T(8,128)}) %reduce-scatter.17.cloned.1.call-update) | async-done | bytes 2097168 | tf_op jit(solution)/shard_map/reduce_scatter | solution.py:190
  574.4 52.1 %all-gather.19.cloned.1.call-done = bf16[1024,2048]{1,0:T(8,128)(2,1)} async-done(((bf16[256,2048]{1,0:T(8,128)(2,1)}), bf16[1024,2048]{1,0:T(8,128)(2,1)}) %all-gather.19.cloned.1.call-update) | async-done | bytes 4194320 | tf_op jit(solution)/shard_map/all_gather | solution.py:164
  626.5 15.5 fusion.190
  655.2 26.0 %all-gather.25.cloned.1.call-done = bf16[1024,2048]{1,0:T(8,128)(2,1)} async-done(((bf16[256,2048]{1,0:T(8,128)(2,1)}), bf16[1024,2048]{1,0:T(8,128)(2,1)}) %all-gather.25.cloned.1.call-update) | async-done | bytes 4194320 | tf_op jit(solution)/shard_map/all_gather | solution.py:177
  681.2 22.1 %multiply_convert_fusion = (bf16[1024,2048]{1,0:T(8,128)(2,1)}, bf16[1024,2048]{1,0:T(8,128)(2,1)}, bf16[1024,2048]{1,0:T(8,128)(2,1)}) fusion(f32[1024,2048]{1,0:T(8,128)} %fusion.189, f32[1024,2048]{1,0:T(8,128)} %fusion.190, bf16[1024,2048]{1,0:T(8,128)(2,1)} %all-gather.25.cloned.1.call-done, bf16[2048,2048]{1,0:T(8,128)(2,1)} %param.22), kind=kOutput, calls=%fused_computation.54 | convolution fusion | flops 8623489024 | bytes 41943040 | tf_op jit(solution)/shard_map/dot_general | solution.py:43
  729.3 14.2 convolution_convert_fusion
  743.6 72.2 %reduce-scatter.21.cloned.1.call-done = f32[256,2048]{1,0:T(8,128)} async-done(((f32[1024,2048]{1,0:T(8,128)}), f32[256,2048]{1,0:T(8,128)}) %reduce-scatter.21.cloned.1.call-update) | async-done | bytes 2097168 | tf_op jit(solution)/shard_map/reduce_scatter | solution.py:190
  819.3 52.2 %reduce-scatter.15.cloned.1.call-done = bf16[256,2048]{1,0:T(8,128)(2,1)} async-done(((bf16[1024,2048]{1,0:T(8,128)(2,1)}), bf16[256,2048]{1,0:T(8,128)(2,1)}) %reduce-scatter.15.cloned.1.call-update) | async-done | bytes 1048592 | tf_op jit(solution)/shard_map/reduce_scatter | solution.py:168
  878.7 52.0 %all-gather.23.cloned.1.call-done = bf16[1024,2048]{1,0:T(8,128)(2,1)} async-done(((bf16[256,2048]{1,0:T(8,128)(2,1)}), bf16[1024,2048]{1,0:T(8,128)(2,1)}) %all-gather.23.cloned.1.call-update) | async-done | bytes 4194320 | tf_op jit(solution)/shard_map/all_gather | solution.py:200
  1030.7 15.0 fusion
  1149.2 15.8 fusion.202
  1188.5 16.5 add_convert_fusion
  1205.1 16.1 add_convert_fusion.1
  1221.2 16.2 add_convert_fusion.2
  1264.2 15.1 all-reduce.2
  1279.5 14.6 all-reduce.3
  1305.6 498.3 %all-reduce.7.cloned.1.call-done = (bf16[128,2048]{1,0:T(8,128)(2,1)}, bf16[128,2048]{1,0:T(8,128)(2,1)}, bf16[512,2048]{1,0:T(8,128)(2,1)}, bf16[2048,2048]{1,0...) async-done(((bf16[128,2048]{1,0:T(8,128)(2,1)}, bf16[128,2048]{1,0:T(8,128)(2,1)}, bf16[512,2048]{1,0:T(8,128)(2,1)}, bf16[2048,2048]{1,0:T(8,128)(2,1)}, ...) | async-done | bytes 28311568 | tf_op jit(solution)/shard_map/psum | solution.py:278
  1847.1 110.2 %all-gather.29.cloned.1.call-done = bf16[4096,2048]{1,0:T(8,128)(2,1)} async-done(((bf16[512,2048]{1,0:T(8,128)(2,1)}), bf16[4096,2048]{1,0:T(8,128)(2,1)}) %all-gather.29.cloned.1.call-update) | async-done | bytes 16777232 | tf_op jit(solution)/shard_map/all_gather | solution.py:86
  (524 shorter events, 616.0 us)
Async XLA Ops:
  7.2 129.4 %copy-start = (bf16[512,2048]{1,0:T(8,128)(2,1)S(1)}, bf16[512,2048]{1,0:T(8,128)(2,1)}, u32[]{:S(2)}) copy-start(bf16[512,2048]{1,0:T(8,128)(2,1)} %param.18) | copy-start | bytes 6291460
  7.2 69.6 %all-gather.17.cloned.1.call-start = ((), (), s32[]{:S(2)}) async-start(), calls=%async_computation.12 | async-start | bytes 5242880 | tf_op jit(solution)/shard_map/all_gather | solution.py:115
  23.7 131.5 %all-gather.13.cloned.1.call-start = ((), (), s32[]{:S(2)}) async-start(), calls=%async_computation.8 | async-start | bytes 5242880 | tf_op jit(solution)/shard_map/all_gather | solution.py:115
  24.4 204.6 %reduce-scatter.13.cloned.1.call-start = ((), (), s32[]{:S(2)}) async-start(), calls=%async_computation.13 | async-start | bytes 10485760 | tf_op jit(solution)/shard_map/reduce_scatter | solution.py:155
  142.3 176.3 %reduce-scatter.9.cloned.1.call-start = ((), (), s32[]{:S(2)}) async-start(), calls=%async_computation.9 | async-start | bytes 10485760 | tf_op jit(solution)/shard_map/reduce_scatter | solution.py:155
  217.1 161.8 %all-gather.15.cloned.1.call-start = ((), (), s32[]{:S(2)}) async-start(), calls=%async_computation.10 | async-start | bytes 5242880 | tf_op jit(solution)/shard_map/all_gather | solution.py:164
  225.8 645.8 %copy-start.68 = (f32[4,1,512]{2,1,0:T(1,128)}, f32[4,1,512]{2,1,0:T(1,128)S(1)}, u32[]{:S(2)}) copy-start(f32[4,1,512]{2,1,0:T(1,128)S(1)} %convert_element_type.371) | copy-start | bytes 24580
  323.5 548.0 %copy-start.91 = (f32[256]{0:T(256)}, f32[256]{0:T(256)S(1)}, u32[]{:S(2)}) copy-start(f32[256]{0:T(256)S(1)} %add_rsqrt_fusion.2) | copy-start | bytes 3076
  326.1 107.9 %all-gather.21.cloned.1.call-start = ((), (), s32[]{:S(2)}) async-start(), calls=%async_computation.16 | async-start | bytes 5242880 | tf_op jit(solution)/shard_map/all_gather | solution.py:177
  329.6 239.0 %reduce-scatter.17.cloned.1.call-start = ((), (), s32[]{:S(2)}) async-start(), calls=%async_computation.17 | async-start | bytes 10485760 | tf_op jit(solution)/shard_map/reduce_scatter | solution.py:190
  482.0 144.5 %all-gather.19.cloned.1.call-start = ((), (), s32[]{:S(2)}) async-start(), calls=%async_computation.14 | async-start | bytes 5242880 | tf_op jit(solution)/shard_map/all_gather | solution.py:164
  482.2 389.3 %copy-start.89 = (f32[256]{0:T(256)}, f32[256]{0:T(256)S(1)}, u32[]{:S(2)}) copy-start(f32[256]{0:T(256)S(1)} %add_rsqrt_fusion) | copy-start | bytes 3076
  573.7 107.6 %all-gather.25.cloned.1.call-start = ((), (), s32[]{:S(2)}) async-start(), calls=%async_computation.20 | async-start | bytes 5242880 | tf_op jit(solution)/shard_map/all_gather | solution.py:177
  574.4 241.5 %reduce-scatter.21.cloned.1.call-start = ((), (), s32[]{:S(2)}) async-start(), calls=%async_computation.21 | async-start | bytes 10485760 | tf_op jit(solution)/shard_map/reduce_scatter | solution.py:190
  729.3 142.3 %reduce-scatter.15.cloned.1.call-start = ((), (), s32[]{:S(2)}) async-start(), calls=%async_computation.15 | async-start | bytes 5242880 | tf_op jit(solution)/shard_map/reduce_scatter | solution.py:168
  743.6 187.2 %all-gather.23.cloned.1.call-start = ((), (), s32[]{:S(2)}) async-start(), calls=%async_computation.18 | async-start | bytes 5242880 | tf_op jit(solution)/shard_map/all_gather | solution.py:200
  743.6 134.2 %copy-start.99 = (f32[256]{0:T(256)}, f32[256]{0:T(256)S(1)}, u32[]{:S(2)}) copy-start(f32[256]{0:T(256)S(1)} %broadcast_multiply_fusion.9) | copy-start | bytes 3076
  819.3 58.7 %copy-start.79 = (f32[2,4,512]{2,1,0:T(4,128)S(1)}, f32[2,4,512]{2,1,0:T(4,128)}, u32[]{:S(2)}) copy-start(f32[2,4,512]{2,1,0:T(4,128)} %copy-done.78) | copy-start | bytes 49156
  877.9 108.2 %all-gather.27.cloned.1.call-start = ((), (), s32[]{:S(2)}) async-start(), calls=%async_computation.22 | async-start | bytes 5242880 | tf_op jit(solution)/shard_map/all_gather | solution.py:200
  878.6 382.6 %reduce-scatter.19.cloned.1.call-start = ((), (), s32[]{:S(2)}) async-start(), calls=%async_computation.19 | async-start | bytes 5242880 | tf_op jit(solution)/shard_map/reduce_scatter | solution.py:255
  1029.8 231.5 %reduce-scatter.23.cloned.1.call-start = ((), (), s32[]{:S(2)}) async-start(), calls=%async_computation.23 | async-start | bytes 5242880 | tf_op jit(solution)/shard_map/reduce_scatter | solution.py:255
  1135.0 160.3 %reduce-scatter.11.cloned.1.call-start = ((), (), s32[]{:S(2)}) async-start(), calls=%async_computation.11 | async-start | bytes 5242880 | tf_op jit(solution)/shard_map/reduce_scatter | solution.py:168
  1149.1 654.8 %all-reduce.7.cloned.1.call-start = ((), (), s32[]{:S(2)}) async-start(), calls=%async_computation.25 | async-start | bytes 56623104 | tf_op jit(solution)/shard_map/psum | solution.py:278
  1250.3 707.0 %all-gather.29.cloned.1.call-start = ((), (), s32[]{:S(2)}) async-start(), calls=%async_computation.24 | async-start | bytes 18874368 | tf_op jit(solution)/shard_map/all_gather | solution.py:86
  (150 other events, 1751.5 us)
Sparse Core Ops, SparseCore 0:
  23.8 52.9 all-gather.16
  79.2 52.6 all-gather.12
  142.4 86.5 reduce-scatter.12
  232.2 86.3 reduce-scatter.8
  326.2 52.6 all-gather.14
  381.2 52.6 all-gather.20
  482.1 86.3 reduce-scatter.16
  573.8 52.6 all-gather.18
  628.5 52.6 all-gather.24
  729.4 86.4 reduce-scatter.20
  818.8 52.6 reduce-scatter.14
  878.0 52.6 all-gather.22
  933.3 52.6 all-gather.26
  1029.9 52.6 reduce-scatter.18
  1135.1 52.6 reduce-scatter.22
  1190.9 52.6 reduce-scatter.10
  1250.4 553.5 all-reduce.6
  1806.0 151.2 all-gather.28
